TPU v7x, 32 devices: a whole 2x2x4 slice. The times are simulated.
32 devices in a mesh: grp: 2 (over x), lon: 16 (over z, y, core).
Axes of the slice: x: 2, y: 2, z: 4, core: 2. Of those that a mesh axis runs over, the one named last changes fastest.
Arguments:
- state: bfloat16 [256, 256, 300], P(None, ('grp', 'lon')), parts along dimension 1, may hold values from -6 to 6
- ocean_mask: int32 [256, 128], P(None, 'lon'), may hold values from 0 to 1, as said below
- fold_map: int32 [128], replicated, may hold values from 0 to 127, as said below
- w_first: bfloat16 [3, 3, 300, 256], replicated, may hold values from -0.125 to 0.125
- b_first: float32 [256], replicated, may hold values from -3 to 3
- w_second: bfloat16 [3, 3, 256, 256], replicated, may hold values from -0.125 to 0.125
- b_second: float32 [256], replicated, may hold values from -3 to 3
Outputs:
- features: bfloat16 [256, 256, 256], P(None, ('grp', 'lon')), parts along dimension 1
There are 2 independent parts, one for each index of `grp`. A program takes and returns all parts, laid end to end along the dimension named above; an argument that names none is the same for every part. Nothing has to cross between parts.
Inputs may be any that keep to these rules, and one draw needn't show every extreme that they name: `ocean_mask`: 1 marks ocean, 0 land; the ocean share varies from column to column. A reflection: (fold_map[i] + i) mod 128 is the same for every i.
All inputs are finite; a program needn't handle non-finite values.
Results may differ from a plain program's by a relative error of at most 0.004.
Values may be sent and summed in bfloat16 or wider, within the bound.
A program may use at most 64 MiB of HBM per device.

v0:
```python
import jax
import jax.numpy as jnp
from jax import lax
from jax.sharding import PartitionSpec as P


def extended(array, sides, width):
    for axis, dim in sides:
        devices, length = (lax.axis_size(axis), array.shape[dim])
        up = [(i, (i + 1) % devices) for i in range(devices)]
        down = [(j, i) for i, j in up]
        last = lax.slice_in_dim(array, length - width, length, axis=dim)
        first = lax.slice_in_dim(array, 0, width, axis=dim)
        before = lax.ppermute(last, axis, up)
        after = lax.ppermute(first, axis, down)
        array = jnp.concatenate([before, array, after], axis=dim)
    return array


def gelu(value):
    return 0.5 * value * (1.0 + jnp.tanh(0.7978845608 * (value + 0.044715 * value * value * value)))


def conv_taps(padded, weight, rows, cols):
    chans = padded.shape[-1]
    total = jnp.zeros((rows * cols, weight.shape[-1]), jnp.float32)
    for shift_y in range(3):
        for shift_x in range(3):
            tap = padded[shift_y : shift_y + rows, shift_x : shift_x + cols].reshape(
                rows * cols, chans
            )
            total = total + jnp.dot(
                tap, weight[shift_y, shift_x], preferred_element_type=jnp.float32
            )
    return total.reshape(rows, cols, weight.shape[-1])


def fold_ghost(gathered, fold_map, start, depth, width):
    total = fold_map.shape[0]
    columns = (start - depth + jnp.arange(width + 2 * depth, dtype=jnp.int32)) % total
    return jnp.take(gathered, jnp.take(fold_map, columns, axis=0), axis=0)


def stack_rows(wide, ghost):
    zeros = jnp.zeros((1,) + wide.shape[1:], wide.dtype)
    return jnp.concatenate([zeros, wide, ghost[None]], axis=0)


def local(state, ocean_mask, fold_map, w_first, b_first, w_second, b_second):
    rows, width, chans = state.shape
    start = lax.axis_index("lon") * width
    masked = state * ocean_mask.astype(jnp.bfloat16)[:, :, None]
    signs = jnp.where(jnp.arange(chans) < chans // 2, -1.0, 1.0).astype(jnp.bfloat16)
    mask_own = ocean_mask.astype(jnp.float32)[:, :, None]
    top_state = lax.all_gather(masked[rows - 1], "lon", axis=0, tiled=True)
    wide = extended(masked, (("lon", 1),), 1)
    ghost = fold_ghost(top_state, fold_map, start, 1, width) * signs
    first = conv_taps(stack_rows(wide, ghost), w_first, rows, width)
    hidden = (gelu(first + b_first) * mask_own).astype(jnp.bfloat16)
    hidden_wide = extended(hidden, (("lon", 1),), 1)
    top_hidden = lax.all_gather(hidden[rows - 1], "lon", axis=0, tiled=True)
    ghost_hidden = fold_ghost(top_hidden, fold_map, start, 1, width)
    second = conv_taps(stack_rows(hidden_wide, ghost_hidden), w_second, rows, width)
    return ((second + b_second) * mask_own).astype(jnp.bfloat16)


def solution(mesh):
    return jax.shard_map(
        local,
        mesh=mesh,
        in_specs=(P(None, ("grp", "lon"), None), P(None, "lon"), P(), P(), P(), P(), P()),
        out_specs=P(None, ("grp", "lon"), None),
        check_vma=False,
    )
```

profile of v0, /device:TPU:0, one launch (start us, length us, event | category | flops | bytes accessed | tf_op | source)
XLA Modules:
  0.0 118.9 jit_solution(11845723673529406524)
XLA Ops:
  0.0 0.8 fusion.94
  0.9 2.4 %copy.28 = bf16[256,8,300]{2,1,0:T(8,128)(2,1)S(1)} copy(bf16[256,8,300]{0,1,2:T(8,128)(2,1)} %param.9) | data formatting | bytes 2457600 | tf_op args[0]
  3.3 0.3 broadcast_multiply_fusion
  3.6 1.3 %fusion.92 = (bf16[256,1,300]{2,1,0:T(2,128)(2,1)S(1)}, bf16[256,1,300]{2,1,0:T(2,128)(2,1)}) fusion(bf16[256,8,300]{2,1,0:T(8,128)(2,1)S(1)} %broadcast_multiply_fusion), kind=kLoop, calls=%fused_computation.138 | loop fusion | bytes 614400 | tf_op jit(solution)/shard_map/slice | solution.py:12
  4.9 0.5 collective-permute-start
  5.3 5.0 %collective-permute-start.1 = (bf16[256,1,300]{2,1,0:T(2,128)(2,1)}, bf16[256,1,300]{2,1,0:T(2,128)(2,1)}, u32[]{:S(2)}, u32[]{:S(2)}) collective-permute-start(bf16[256,1,300]{2,1,0:T(2,128)(2,1)} %get-tuple-element.17), channel_id=1, source_target_pairs={{1,0},{2,1},{3,2},{4,3},{5,4},{6,5},{7,6},{8,7},{9,8},{10,9},{11,1... | collective-permute-start | bytes 460808 | tf_op jit(solution)/shard_map/ppermute | solution.py:15
  10.4 1.1 copy.30
  11.5 20.3 %all-gather = bf16[1,128,300]{2,1,0:T(8,128)(2,1)S(1)} all-gather(bf16[1,8,300]{2,1,0:T(8,128)(2,1)S(1)} %slice.187), channel_id=2, replica_groups=mesh['grp'=2,'lon'=16] {'lon'}, dimensions={1}, use_global_device_ids=true | all-gather | bytes 81600 | tf_op jit(solution)/shard_map/all_gather | solution.py:55
  31.9 0.7 gather_fusion.2
  32.6 0.6 gather_fusion
  33.2 1.2 %copy.41 = bf16[1,10,300]{0,2,1:T(8,128)(2,1)} copy(bf16[1,10,300]{2,1,0:T(8,128)(2,1)S(1)} %fusion.82) | data formatting | bytes 12000 | tf_op jit(solution)/shard_map/mul | solution.py:57
  34.7 1.2 %copy.29 = bf16[256,1,300]{0,2,1:T(8,128)(2,1)S(1)} copy(bf16[256,1,300]{2,1,0:T(2,128)(2,1)} %collective-permute-done) | data formatting | bytes 307200 | tf_op jit(solution)/shard_map/ppermute | solution.py:14
  36.0 1.2 %copy.31 = bf16[256,1,300]{0,2,1:T(8,128)(2,1)S(1)} copy(bf16[256,1,300]{2,1,0:T(2,128)(2,1)} %collective-permute-done.1) | data formatting | bytes 307200 | tf_op jit(solution)/shard_map/ppermute | solution.py:15
  37.2 1.7 %pad_maximum_fusion.2 = (bf16[256,8,300]{0,2,1:T(8,128)(2,1)}, bf16[256,8,300]{0,2,1:T(8,128)(2,1)}) fusion(bf16[256,1,300]{0,2,1:T(8,128)(2,1)S(1)} %copy.31, bf16[256,8,300]{0,2,1:T(8,128)(2,1)S(1)} %copy.30, bf16[256,1,300]{0,2,1:T(8,128)(2,1)S(1)} %copy.29), kind=kLoop, calls=%fused_computation.61 | loop fusion | flops 1228800 | bytes 3993600 | tf_op jit(solution)/shard_map/concatenate | solution.py:16
  38.9 2.0 %pad_maximum_fusion = (bf16[257,10,300]{0,2,1:T(8,128)(2,1)S(1)}, bf16[257,10,300]{0,2,1:T(8,128)(2,1)S(1)}) fusion(bf16[1,10,300]{0,2,1:T(8,128)(2,1)S(1)} %copy-done.11, bf16[256,1,300]{0,2,1:T(8,128)(2,1)S(1)} %copy.31, bf16[256,8,300]{0,2,1:T(8,128)(2,1)S(1)} %copy.30, bf16[256,1,300]{0,2,1:T(8,128)(2,1)S(1)} %copy.29), kind=kLoop, calls=%fused_computation.31 | loop fusion | flops 13878000 | bytes 4626000 | tf_op jit(solution)/shard_map/concatenate | solution.py:46
  41.0 3.8 %fusion.90 = (bf16[256,8,300]{0,2,1:T(8,128)(2,1)}, bf16[256,8,300]{0,2,1:T(8,128)(2,1)}, bf16[256,8,300]{0,2,1:T(8,128)(2,1)}, bf16[256,8,300]{0,2,1:T(8,128)(2...) fusion(bf16[257,10,300]{0,2,1:T(8,128)(2,1)S(1)} %get-tuple-element.18, ...), kind=kLoop, calls=%fused_computation.136 | loop fusion | bytes 14745600 | tf_op jit(solution)/shard_map/slice | solution.py:29
  44.7 2.9 %copy.32 = bf16[256,8,300]{2,1,0:T(8,128)(2,1)} copy(bf16[256,8,300]{0,2,1:T(8,128)(2,1)} %get-tuple-element.28) | data formatting | bytes 2457600 | tf_op jit(solution)/shard_map/slice | solution.py:29
  47.6 2.9 %copy.33 = bf16[256,8,300]{2,1,0:T(8,128)(2,1)} copy(bf16[256,8,300]{0,2,1:T(8,128)(2,1)} %get-tuple-element.29) | data formatting | bytes 2457600 | tf_op jit(solution)/shard_map/slice | solution.py:29
  50.5 2.0 %copy.34 = bf16[256,8,300]{2,1,0:T(8,128)(2,1)} copy(bf16[256,8,300]{0,2,1:T(8,128)(2,1)S(1)} %get-tuple-element.30) | data formatting | bytes 2457600 | tf_op jit(solution)/shard_map/slice | solution.py:29
  52.5 2.1 %copy.37 = bf16[256,8,300]{2,1,0:T(8,128)(2,1)S(1)} copy(bf16[256,8,300]{0,2,1:T(8,128)(2,1)} %get-tuple-element.21) | data formatting | bytes 2457600 | tf_op jit(solution)/shard_map/slice | solution.py:29
  54.7 2.2 %fusion.34 = f32[2048,256]{1,0:T(8,128)S(1)} fusion(bf16[256,8,300]{2,1,0:T(8,128)(2,1)} %copy.32, bf16[3,3,300,256]{3,2,1,0:T(8,128)(2,1)} %param.12), kind=kOutput, calls=%fused_computation.59 | convolution fusion | flops 314572800 | bytes 3825664 | tf_op jit(solution)/shard_map/dot_general | solution.py:32
  56.9 1.7 %convolution_add_fusion.7 = f32[2048,256]{1,0:T(8,128)S(1)} fusion(f32[2048,256]{1,0:T(8,128)S(1)} %fusion.34, bf16[256,8,300]{2,1,0:T(8,128)(2,1)S(1)} %copy-done.6, bf16[3,3,300,256]{3,2,1,0:T(8,128)(2,1)} %param.12), kind=kOutput, calls=%fused_computation.20 | convolution fusion | flops 315097088 | bytes 5578752 | tf_op jit(solution)/shard_map/dot_general | solution.py:32
  58.7 1.6 %convolution_add_fusion.6 = f32[2048,256]{1,0:T(8,128)S(1)} fusion(f32[2048,256]{1,0:T(8,128)S(1)} %convolution_add_fusion.7, bf16[256,8,300]{2,1,0:T(8,128)(2,1)S(1)} %copy-done.5, bf16[3,3,300,256]{3,2,1,0:T(8,128)(2,1)} %param.12), kind=kOutput, calls=%fused_computation.19 | convolution fusion | flops 315097088 | bytes 5578752 | tf_op jit(solution)/shard_map/dot_general | solution.py:32
  60.3 1.6 %convolution_add_fusion.5 = f32[2048,256]{1,0:T(8,128)S(1)} fusion(f32[2048,256]{1,0:T(8,128)S(1)} %convolution_add_fusion.6, bf16[256,8,300]{2,1,0:T(8,128)(2,1)S(1)} %copy.37, bf16[3,3,300,256]{3,2,1,0:T(8,128)(2,1)} %param.12), kind=kOutput, calls=%fused_computation.18 | convolution fusion | flops 315097088 | bytes 5578752 | tf_op jit(solution)/shard_map/dot_general | solution.py:32
  61.9 3.1 %convolution_add_fusion.4 = f32[2048,256]{1,0:T(8,128)} fusion(f32[2048,256]{1,0:T(8,128)S(1)} %convolution_add_fusion.5, bf16[256,8,300]{2,1,0:T(8,128)(2,1)S(1)} %broadcast_multiply_fusion, bf16[3,3,300,256]{3,2,1,0:T(8,128)(2,1)} %param.12), kind=kOutput, calls=%fused_computation.17 | convolution fusion | flops 315097088 | bytes 5578752 | tf_op jit(solution)/shard_map/dot_general | solution.py:32
  65.0 2.0 %copy.40 = bf16[256,8,300]{2,1,0:T(8,128)(2,1)} copy(bf16[256,8,300]{0,2,1:T(8,128)(2,1)S(1)} %copy-done.10) | data formatting | bytes 2457600 | tf_op jit(solution)/shard_map/slice | solution.py:29
  67.1 2.1 %copy.42 = bf16[256,8,300]{2,1,0:T(8,128)(2,1)} copy(bf16[256,8,300]{0,2,1:T(8,128)(2,1)S(1)} %copy-done.9) | data formatting | bytes 2457600 | tf_op jit(solution)/shard_map/slice | solution.py:29
  69.1 2.0 %copy.43 = bf16[256,8,300]{2,1,0:T(8,128)(2,1)} copy(bf16[256,8,300]{0,2,1:T(8,128)(2,1)S(1)} %copy-done.8) | data formatting | bytes 2457600 | tf_op jit(solution)/shard_map/slice | solution.py:29
  71.2 2.1 %copy.44 = bf16[256,8,300]{2,1,0:T(8,128)(2,1)} copy(bf16[256,8,300]{0,2,1:T(8,128)(2,1)S(1)} %copy-done.7) | data formatting | bytes 2457600 | tf_op jit(solution)/shard_map/slice | solution.py:29
  73.3 2.2 %convolution_add_fusion.3 = f32[2048,256]{1,0:T(8,128)S(1)} fusion(f32[2048,256]{1,0:T(8,128)S(1)} %copy-done.2, bf16[256,8,300]{2,1,0:T(8,128)(2,1)} %copy.40, bf16[3,3,300,256]{3,2,1,0:T(8,128)(2,1)} %param.12), kind=kOutput, calls=%fused_computation.16 | convolution fusion | flops 315097088 | bytes 5922816 | tf_op jit(solution)/shard_map/dot_general | solution.py:32
  75.6 1.7 %convolution_add_fusion.2 = f32[2048,256]{1,0:T(8,128)S(1)} fusion(f32[2048,256]{1,0:T(8,128)S(1)} %convolution_add_fusion.3, bf16[256,8,300]{2,1,0:T(8,128)(2,1)S(1)} %copy-done.4, bf16[3,3,300,256]{3,2,1,0:T(8,128)(2,1)} %param.12), kind=kOutput, calls=%fused_computation.15 | convolution fusion | flops 315097088 | bytes 5578752 | tf_op jit(solution)/shard_map/dot_general | solution.py:32
  77.3 1.7 %convolution_add_fusion.1 = f32[2048,256]{1,0:T(8,128)S(1)} fusion(f32[2048,256]{1,0:T(8,128)S(1)} %convolution_add_fusion.2, bf16[256,8,300]{2,1,0:T(8,128)(2,1)S(1)} %copy-done.3, bf16[3,3,300,256]{3,2,1,0:T(8,128)(2,1)} %param.12), kind=kOutput, calls=%fused_computation.14 | convolution fusion | flops 315097088 | bytes 5578752 | tf_op jit(solution)/shard_map/dot_general | solution.py:32
  79.1 3.5 %fusion.17 = (bf16[256,8,256]{2,1,0:T(8,128)(2,1)S(1)}, f32[2048,256]{1,0:T(8,128)}) fusion(f32[256,8]{1,0:T(8,128)S(1)} %copy.45, f32[256]{0:T(256)S(1)} %copy-done.14, f32[2048,256]{1,0:T(8,128)S(1)} %convolution_add_fusion.1, bf16[3,3,300,256]{3,2,1,0:T(8,128)(2,1)} %param.12, bf16[256,8,300]{2,1,0:T(8,128)(2,1)S(1)} %copy-done.12), kind=kOutput, calls=%fused_computation.40 | convolution fusion | flops 320864256 | bytes 6636544 | tf_op jit(solution)/shard_map/dot_general | solution.py:32
  82.5 0.3 fusion.93
  82.9 0.4 collective-permute-start.2
  83.3 4.1 %collective-permute-start.3 = (bf16[256,1,256]{2,1,0:T(2,128)(2,1)S(1)}, bf16[256,1,256]{2,1,0:T(2,128)(2,1)S(1)}, u32[]{:S(2)}, u32[]{:S(2)}) collective-permute-start(bf16[256,1,256]{2,1,0:T(2,128)(2,1)S(1)} %get-tuple-element.23), channel_id=1, source_target_pairs={{1,0},{2,1},{3,2},{4,3},{5,4},{6,5},{7,6},{8,7},{9,8},{10,9},{11,1... | collective-permute-start | bytes 393224 | tf_op jit(solution)/shard_map/ppermute | solution.py:15
  87.4 19.5 %all-gather.1 = bf16[1,128,256]{2,1,0:T(8,128)(2,1)S(1)} all-gather(bf16[1,8,256]{2,1,0:T(8,128)(2,1)S(1)} %slice.196), channel_id=3, replica_groups=mesh['grp'=2,'lon'=16] {'lon'}, dimensions={1}, use_global_device_ids=true | all-gather | bytes 69632 | tf_op jit(solution)/shard_map/all_gather | solution.py:61
  106.9 0.6 gather_fusion.1
  107.4 2.5 %fusion.44 = f32[2048,256]{1,0:T(8,128)S(1)} fusion(f32[2048,256]{1,0:T(8,128)} %get-tuple-element.27, f32[2048]{0:T(1024)S(1)} %mul.123, f32[256]{0:T(256)S(1)} %copy-done.14, bf16[3,3,256,256]{3,2,1,0:T(8,128)(2,1)S(1)} %copy-done.13), kind=kOutput, calls=%fused_computation.77 | convolution fusion | flops 274202624 | bytes 4334592 | tf_op jit(solution)/shard_map/dot_general | solution.py:32
  110.1 2.8 %fusion.11 = (bf16[257,10,256]{2,1,0:T(8,128)(2,1)S(1)}, bf16[257,10,256]{2,1,0:T(8,128)(2,1)S(1)}) fusion(bf16[256,1,256]{2,1,0:T(2,128)(2,1)S(1)} %collective-permute-done.3, bf16[256,8,256]{2,1,0:T(8,128)(2,1)S(1)} %get-tuple-element.26, bf16[256,1,256]{2,1,0:T(2,128)(2,1)S(1)} %collective-permute-done.2, bf16[1,10,256]{2,1,0:T(8,128)(2,1)S(1)} %bitcast_select_fusion.1), kind=kLoop, calls=%fused_computation.33 | loop fusion | flops 11842560 | bytes 3947520 | tf_op jit(solution)/shard_map/concatenate | solution.py:16
  112.9 0.4 fusion.43
  113.3 0.5 convolution_add_fusion.13
  113.9 0.5 convolution_add_fusion.12
  114.4 0.4 fusion.36
  114.8 0.8 fusion.7
  115.6 0.9 fusion.6
  116.6 0.5 convolution_add_fusion.9
  117.2 1.7 %fusion.25 = bf16[256,8,256]{2,1,0:T(8,128)(2,1)} fusion(f32[2048,256]{1,0:T(8,128)S(1)} %convolution_add_fusion.9, bf16[257,10,256]{2,1,0:T(8,128)(2,1)S(1)} %get-tuple-element.15, f32[256]{0:T(256)S(1)} %copy-done.15, f32[256,8]{1,0:T(8,128)S(1)} %copy.45, bf16[3,3,256,256]{3,2,1,0:T(8,128)(2,1)S(1)} %copy-done.13), kind=kOutput, calls=%fused_computation.49 | convolution fusion | flops 270532608 | bytes 4457472 | tf_op jit(solution)/shard_map/dot_general | solution.py:32
  (48 shorter events, 0.8 us)
Async XLA Ops:
  0.0 31.9 %copy-start = (s32[128]{0:T(128)S(1)}, s32[128]{0:T(128)}, u32[]{:S(2)}) copy-start(s32[128]{0:T(128)} %param.11) | copy-start | bytes 1540
  4.9 29.8 %collective-permute-start = (bf16[256,1,300]{2,1,0:T(2,128)(2,1)S(1)}, bf16[256,1,300]{2,1,0:T(2,128)(2,1)}, u32[]{:S(2)}, u32[]{:S(2)}) collective-permute-start(bf16[256,1,300]{2,1,0:T(2,128)(2,1)S(1)} %get-tuple-element.16), channel_id=1, source_target_pairs={{0,1},{1,2},{2,3},{3,4},{4,5},{5,6},{6,7},{7,8},{8,9},{9,10},{10,1... | collective-permute-start | bytes 460808 | tf_op jit(solution)/shard_map/ppermute | solution.py:14
  5.3 30.6 %collective-permute-start.1 = (bf16[256,1,300]{2,1,0:T(2,128)(2,1)}, bf16[256,1,300]{2,1,0:T(2,128)(2,1)}, u32[]{:S(2)}, u32[]{:S(2)}) collective-permute-start(bf16[256,1,300]{2,1,0:T(2,128)(2,1)} %get-tuple-element.17), channel_id=1, source_target_pairs={{1,0},{2,1},{3,2},{4,3},{5,4},{6,5},{7,6},{8,7},{9,8},{10,9},{11,1... | collective-permute-start | bytes 460808 | tf_op jit(solution)/shard_map/ppermute | solution.py:15
  37.2 1.7 %copy-start.11 = (bf16[1,10,300]{0,2,1:T(8,128)(2,1)S(1)}, bf16[1,10,300]{0,2,1:T(8,128)(2,1)}, u32[]{:S(2)}) copy-start(bf16[1,10,300]{0,2,1:T(8,128)(2,1)} %copy.41) | copy-start | bytes 18004
  54.7 2.2 %copy-start.6 = (bf16[256,8,300]{2,1,0:T(8,128)(2,1)S(1)}, bf16[256,8,300]{2,1,0:T(8,128)(2,1)}, u32[]{:S(2)}) copy-start(bf16[256,8,300]{2,1,0:T(8,128)(2,1)} %copy.33) | copy-start | bytes 3686404
  56.9 1.8 %copy-start.5 = (bf16[256,8,300]{2,1,0:T(8,128)(2,1)S(1)}, bf16[256,8,300]{2,1,0:T(8,128)(2,1)}, u32[]{:S(2)}) copy-start(bf16[256,8,300]{2,1,0:T(8,128)(2,1)} %copy.34) | copy-start | bytes 3686404
  61.9 3.1 %copy-start.10 = (bf16[256,8,300]{0,2,1:T(8,128)(2,1)S(1)}, bf16[256,8,300]{0,2,1:T(8,128)(2,1)}, u32[]{:S(2)}) copy-start(bf16[256,8,300]{0,2,1:T(8,128)(2,1)} %get-tuple-element.20) | copy-start | bytes 3686404
  65.0 2.0 %copy-start.9 = (bf16[256,8,300]{0,2,1:T(8,128)(2,1)S(1)}, bf16[256,8,300]{0,2,1:T(8,128)(2,1)}, u32[]{:S(2)}) copy-start(bf16[256,8,300]{0,2,1:T(8,128)(2,1)} %get-tuple-element.10) | copy-start | bytes 3686404
  67.1 2.1 %copy-start.8 = (bf16[256,8,300]{0,2,1:T(8,128)(2,1)S(1)}, bf16[256,8,300]{0,2,1:T(8,128)(2,1)}, u32[]{:S(2)}) copy-start(bf16[256,8,300]{0,2,1:T(8,128)(2,1)} %get-tuple-element.9) | copy-start | bytes 3686404
  69.1 2.0 %copy-start.7 = (bf16[256,8,300]{0,2,1:T(8,128)(2,1)S(1)}, bf16[256,8,300]{0,2,1:T(8,128)(2,1)}, u32[]{:S(2)}) copy-start(bf16[256,8,300]{0,2,1:T(8,128)(2,1)} %get-tuple-element.8) | copy-start | bytes 3686404
  71.2 2.1 %copy-start.2 = (f32[2048,256]{1,0:T(8,128)S(1)}, f32[2048,256]{1,0:T(8,128)}, u32[]{:S(2)}) copy-start(f32[2048,256]{1,0:T(8,128)} %convolution_add_fusion.4) | copy-start | bytes 6291460
  73.3 2.2 %copy-start.4 = (bf16[256,8,300]{2,1,0:T(8,128)(2,1)S(1)}, bf16[256,8,300]{2,1,0:T(8,128)(2,1)}, u32[]{:S(2)}) copy-start(bf16[256,8,300]{2,1,0:T(8,128)(2,1)} %copy.42) | copy-start | bytes 3686404
  75.5 1.8 %copy-start.3 = (bf16[256,8,300]{2,1,0:T(8,128)(2,1)S(1)}, bf16[256,8,300]{2,1,0:T(8,128)(2,1)}, u32[]{:S(2)}) copy-start(bf16[256,8,300]{2,1,0:T(8,128)(2,1)} %copy.43) | copy-start | bytes 3686404
  77.3 1.8 %copy-start.12 = (bf16[256,8,300]{2,1,0:T(8,128)(2,1)S(1)}, bf16[256,8,300]{2,1,0:T(8,128)(2,1)}, u32[]{:S(2)}) copy-start(bf16[256,8,300]{2,1,0:T(8,128)(2,1)} %copy.44) | copy-start | bytes 3686404
  77.3 1.8 %copy-start.14 = (f32[256]{0:T(256)S(1)}, f32[256]{0:T(256)}, u32[]{:S(2)}) copy-start(f32[256]{0:T(256)} %param.13) | copy-start | bytes 3076
  79.1 28.4 %copy-start.13 = (bf16[3,3,256,256]{3,2,1,0:T(8,128)(2,1)S(1)}, bf16[3,3,256,256]{3,2,1,0:T(8,128)(2,1)}, u32[]{:S(2)}) copy-start(bf16[3,3,256,256]{3,2,1,0:T(8,128)(2,1)} %param.14) | copy-start | bytes 3538948
  82.9 27.1 %collective-permute-start.2 = (bf16[256,1,256]{2,1,0:T(2,128)(2,1)S(1)}, bf16[256,1,256]{2,1,0:T(2,128)(2,1)S(1)}, u32[]{:S(2)}, u32[]{:S(2)}) collective-permute-start(bf16[256,1,256]{2,1,0:T(2,128)(2,1)S(1)} %get-tuple-element.22), channel_id=1, source_target_pairs={{0,1},{1,2},{2,3},{3,4},{4,5},{5,6},{6,7},{7,8},{8,9},{9,10},{10,1... | collective-permute-start | bytes 393224 | tf_op jit(solution)/shard_map/ppermute | solution.py:14
  83.3 26.7 %collective-permute-start.3 = (bf16[256,1,256]{2,1,0:T(2,128)(2,1)S(1)}, bf16[256,1,256]{2,1,0:T(2,128)(2,1)S(1)}, u32[]{:S(2)}, u32[]{:S(2)}) collective-permute-start(bf16[256,1,256]{2,1,0:T(2,128)(2,1)S(1)} %get-tuple-element.23), channel_id=1, source_target_pairs={{1,0},{2,1},{3,2},{4,3},{5,4},{6,5},{7,6},{8,7},{9,8},{10,9},{11,1... | collective-permute-start | bytes 393224 | tf_op jit(solution)/shard_map/ppermute | solution.py:15
  116.5 0.7 copy-start.15
  116.5 2.3 %copy-start.1 = (s32[128]{0:T(128)S(1)}, s32[128]{0:T(128)}, u32[]{:S(2)}) copy-start(s32[128]{0:T(128)} %param.11) | copy-start | bytes 1540
where the time goes:
time: 119 us
  blocking collectives  39.8 us (33%)
  local copies, waits for them, and re-layouts  33.1 us (28%)
  matrix products  27.8 us (23%)
  starting transfers between devices  9.94 us (8%)
  other arithmetic  7.89 us (7%)
    dot_general x18, matrix products, conv_taps(): jnp.dot(tap, weight[shift_y, shift_x], preferred_element_type=jnp.float32)  27.8 us
    slice x9, local copies, waits for them, and re-layouts, conv_taps(): padded[shift_y:shift_y + rows, shift_x:shift_x + cols]  21.9 us
    all_gather x1, blocking collectives, local(): top_state = lax.all_gather(masked[rows - 1], 'lon', axis=0, tiled=True)  20.3 us
    all_gather x1, blocking collectives, local(): top_hidden = lax.all_gather(hidden[rows - 1], 'lon', axis=0, tiled=True)  19.5 us
    ppermute x2, starting transfers between devices, extended(): after = lax.ppermute(first, axis, down)  9.09 us
    concatenate x2, other arithmetic, extended(): array = jnp.concatenate([before, array, after], axis=dim)  4.51 us
    unnamed x33, local copies, waits for them, and re-layouts  2.55 us
  transfers between devices with their start and end apart: 4, of which 0 were waited for; matrix products, arithmetic and copies ran while one was open for 7% of the time, Pallas kernels for 0%

commit v1 on v0

v1 whole, which is shorter than its diff:
```python
import functools

import jax
import jax.numpy as jnp
from jax import lax
from jax.experimental import pallas as pl
from jax.experimental.pallas import tpu as pltpu
from jax.sharding import PartitionSpec as P

LANES = 128
TAIL_SLOT = 64
MESH = pl.DeviceIdType.MESH
F32 = jnp.float32
BF16 = jnp.bfloat16


def gelu(value):
    return 0.5 * value * (1.0 + jnp.tanh(0.7978845608 * (value + 0.044715 * value * value * value)))


def kernel(
    x_hbm, m_ref, fold_ref, w1_hbm, b1_ref, w2_hbm, b2_ref, out_ref,
    xv, xs, w1, w2, wt, cols1, tails, cols2, top1, top2, mcol,
    load_sem, t1_send, t1_recv, t2_send, t2_recv, x_send, x_recv, h_send, h_recv,
):
    n = lax.axis_size("lon")
    me = lax.axis_index("lon")
    right, left = lax.rem(me + 1, n), lax.rem(me + n - 1, n)
    chans, width, rows = x_hbm.shape
    main = w1.shape[-1]
    hid = w2.shape[-1]
    padded = main + LANES
    total = n * width

    barrier = pltpu.get_barrier_semaphore()

    def greet(i, _):
        pl.semaphore_signal(
            barrier, inc=1, device_id={"lon": lax.rem(me + i, n)}, device_id_type=MESH
        )
        return 0

    lax.fori_loop(1, n, greet, 0)
    load_x = pltpu.make_async_copy(x_hbm, xv, load_sem.at[0])
    load_1 = pltpu.make_async_copy(w1_hbm, w1, load_sem.at[1])
    load_2 = pltpu.make_async_copy(w2_hbm, w2, load_sem.at[2])
    load_x.start()
    load_1.start()
    load_2.start()

    wt[...] = jnp.zeros_like(wt)
    halves = rows // LANES
    for h in range(halves):
        xs[h, chans * width :, :] = jnp.zeros((xs.shape[1] - chans * width, LANES), F32)
    mask = m_ref[...].astype(F32)
    mask_t = jnp.transpose(jnp.concatenate([mask] * (LANES // width), axis=0))
    for c in range(width):
        mcol[c] = mask_t[:, c : c + 1]
    row = lax.broadcasted_iota(jnp.int32, (rows, 1), 0)
    first_row, last_row = row == 0, row == rows - 1
    last_tile = lax.broadcasted_iota(jnp.int32, (16, 1), 0) == 15

    def build1(slot, value):
        up = jnp.where(first_row, 0.0, pltpu.roll(value, 1, 0))
        down = jnp.where(last_row, 0.0, pltpu.roll(value, rows - 1, 0))
        cols1[slot, :, 0:main] = up[:, :main].astype(BF16)
        cols1[slot, :, 2 * main : 3 * main] = down[:, :main].astype(BF16)
        pair = up[:, main:] + pltpu.roll(value[:, main:], TAIL_SLOT, 1)
        cols1[slot, :, 3 * main : 3 * main + LANES] = pair.astype(BF16)
        cols1[slot, :, 3 * main + LANES :] = down[:, main:].astype(BF16)

    def build2(slot, value):
        up = jnp.where(first_row, 0.0, pltpu.roll(value, 1, 0))
        down = jnp.where(last_row, 0.0, pltpu.roll(value, rows - 1, 0))
        cols2[slot, :, 0:hid] = up.astype(BF16)
        cols2[slot, :, 2 * hid : 3 * hid] = down.astype(BF16)

    def patch(buffer, slot, lo, hi, ghost):
        old = buffer[slot, rows - 16 :, lo:hi].astype(F32)
        buffer[slot, rows - 16 :, lo:hi] = jnp.where(last_tile, ghost, old).astype(BF16)

    def folded(top, slot):
        column = lax.rem(me * width + slot - 1 + total, total)
        return top[pl.ds(fold_ref[column], 1), :]

    signs = jnp.where(
        lax.broadcasted_iota(jnp.int32, (1, padded), 1) < chans // 2, -1.0, 1.0
    )

    def fold1(slot, _):
        ghost = folded(top1, slot) * signs
        patch(cols1, slot, 2 * main, 3 * main, ghost[:, :main])
        patch(cols1, slot, 3 * main + LANES, 3 * main + 2 * LANES, ghost[:, main:])
        return 0

    def fold2(slot, _):
        patch(cols2, slot, 2 * hid, 3 * hid, folded(top2, slot))
        return 0

    def top_copy(top, send, recv, i):
        peer = lax.rem(me + i, n)
        block = pl.ds(pl.multiple_of(me * width, width), width)
        return pltpu.make_async_remote_copy(
            src_ref=top.at[block], dst_ref=top.at[block], send_sem=send.at[i],
            recv_sem=recv.at[i], device_id={"lon": peer}, device_id_type=MESH,
        )

    def send_tops(top, send, recv):
        def one(i, _):
            top_copy(top, send, recv, i).start()
            return 0

        lax.fori_loop(1, n, one, 0)

    def wait_tops(top, send, recv):
        def one(i, _):
            top_copy(top, send, recv, i).wait()
            return 0

        lax.fori_loop(1, n, one, 0)

    def halo(src, dst, send, recv, k, peer):
        return pltpu.make_async_remote_copy(
            src_ref=src, dst_ref=dst, send_sem=send.at[k], recv_sem=recv.at[k],
            device_id={"lon": peer}, device_id_type=MESH,
        )

    load_x.wait()
    masked = (xv[...].astype(F32) * mask[None]).reshape(chans * width, rows)
    for h in range(halves):
        xs[h, 0 : chans * width, :] = masked[:, h * LANES : (h + 1) * LANES]

    def spread(c, _):
        value = jnp.concatenate(
            [jnp.transpose(xs[h, pl.ds(c, padded, stride=width), :]) for h in range(halves)], axis=0
        )
        cols1[c + 1, :, main : 2 * main] = value[:, :main].astype(BF16)
        tails[c + 1] = value[:, main:].astype(BF16)
        top1[pl.ds(me * width + c, 1), :] = value[rows - 1 :, :]
        build1(c + 1, value)
        return 0

    lax.fori_loop(0, width, spread, 0)
    pl.semaphore_wait(barrier, n - 1)
    send_tops(top1, t1_send, t1_recv)
    mid1, mid2 = pl.ds(main, main), pl.ds(hid, hid)
    x_halos = [
        halo(cols1.at[1, :, mid1], cols1.at[width + 1, :, mid1], x_send, x_recv, 0, left),
        halo(tails.at[1], tails.at[width + 1], x_send, x_recv, 1, left),
        halo(cols1.at[width, :, mid1], cols1.at[0, :, mid1], x_send, x_recv, 2, right),
        halo(tails.at[width], tails.at[0], x_send, x_recv, 3, right),
    ]
    for copy in x_halos:
        copy.start()

    load_1.wait()
    for dx in range(3):
        for dy in range(3):
            wt[dx, TAIL_SLOT * dy : TAIL_SLOT * dy + chans - main, :] = w1[dy, dx, main:chans, :]

    wait_tops(top1, t1_send, t1_recv)
    lax.fori_loop(1, width + 1, fold1, 0)

    def first(ca, cb):
        acc = None
        for dx in range(3):
            lhs = jnp.concatenate([cols1[ca + dx], cols1[cb + dx]], axis=0)
            rhs = jnp.concatenate([w1[dy, dx, :main, :] for dy in range(3)] + [wt[dx]], axis=0)
            part = jnp.dot(lhs, rhs, preferred_element_type=F32)
            acc = part if acc is None else acc + part
        for k, c in enumerate((ca, cb)):
            value = gelu(acc[k * rows : (k + 1) * rows] + b1_ref[...]) * mcol[c]
            value = value.astype(BF16)
            cols2[c + 1, :, hid : 2 * hid] = value
            value = value.astype(F32)
            top2[pl.ds(me * width + c, 1), :] = value[rows - 1 :, :]
            build2(c + 1, value)

    def second(ca, cb):
        acc = None
        for dx in range(3):
            lhs = jnp.concatenate([cols2[ca + dx], cols2[cb + dx]], axis=0)
            rhs = jnp.concatenate([w2[dy, dx] for dy in range(3)], axis=0)
            part = jnp.dot(lhs, rhs, preferred_element_type=F32)
            acc = part if acc is None else acc + part
        for k, c in enumerate((ca, cb)):
            value = (acc[k * rows : (k + 1) * rows] + b2_ref[...]) * mcol[c]
            out_ref[c] = value.astype(BF16)

    def inner(step):
        def one(i, _):
            step(2 * i + 1, 2 * i + 2)
            return 0

        lax.fori_loop(0, (width - 2) // 2, one, 0)

    inner(first)
    for copy in x_halos:
        copy.wait()
    for slot in (0, width + 1):
        mid = jnp.concatenate([cols1[slot, :, main : 2 * main], tails[slot]], axis=1)
        build1(slot, mid.astype(F32))
        fold1(slot, 0)
    first(0, width - 1)

    send_tops(top2, t2_send, t2_recv)
    h_halos = [
        halo(cols2.at[1, :, mid2], cols2.at[width + 1, :, mid2], h_send, h_recv, 0, left),
        halo(cols2.at[width, :, mid2], cols2.at[0, :, mid2], h_send, h_recv, 1, right),
    ]
    for copy in h_halos:
        copy.start()
    load_2.wait()
    wait_tops(top2, t2_send, t2_recv)
    lax.fori_loop(1, width + 1, fold2, 0)
    inner(second)
    for copy in h_halos:
        copy.wait()
    for slot in (0, width + 1):
        build2(slot, cols2[slot, :, hid : 2 * hid].astype(F32))
        fold2(slot, 0)
    second(0, width - 1)


def local(n, state, ocean_mask, fold_map, w_first, b_first, w_second, b_second):
    rows, width, chans = state.shape
    hid = w_first.shape[-1]
    out = w_second.shape[-1]
    main = chans // LANES * LANES
    vmem = pl.BlockSpec(memory_space=pltpu.VMEM)
    hbm = pl.BlockSpec(memory_space=pl.ANY)
    result = pl.pallas_call(
        kernel,
        out_shape=jax.ShapeDtypeStruct((width, rows, out), BF16),
        in_specs=[hbm, vmem, pl.BlockSpec(memory_space=pltpu.SMEM), hbm, vmem, hbm, vmem],
        out_specs=vmem,
        scratch_shapes=[
            pltpu.VMEM((chans, width, rows), BF16),
            pltpu.VMEM((rows // LANES, (main + LANES) * width, LANES), F32),
            pltpu.VMEM(w_first.shape, BF16),
            pltpu.VMEM(w_second.shape, BF16),
            pltpu.VMEM((3, 2 * LANES, hid), BF16),
            pltpu.VMEM((width + 2, rows, 3 * main + 2 * LANES), BF16),
            pltpu.VMEM((width + 2, rows, LANES), BF16),
            pltpu.VMEM((width + 2, rows, 3 * hid), BF16),
            pltpu.VMEM((n * width, main + LANES), F32),
            pltpu.VMEM((n * width, hid), F32),
            pltpu.VMEM((width, rows, 1), F32),
            pltpu.SemaphoreType.DMA((3,)),
            pltpu.SemaphoreType.DMA((n,)),
            pltpu.SemaphoreType.DMA((n,)),
            pltpu.SemaphoreType.DMA((n,)),
            pltpu.SemaphoreType.DMA((n,)),
            pltpu.SemaphoreType.DMA((4,)),
            pltpu.SemaphoreType.DMA((4,)),
            pltpu.SemaphoreType.DMA((2,)),
            pltpu.SemaphoreType.DMA((2,)),
        ],
        compiler_params=pltpu.CompilerParams(
            collective_id=0, has_side_effects=True, vmem_limit_bytes=56 * 1024 * 1024
        ),
        name="masked_conv_pair",
    )(
        jnp.transpose(state, (2, 1, 0)),
        jnp.transpose(ocean_mask),
        fold_map,
        w_first,
        b_first.reshape(1, hid),
        w_second,
        b_second.reshape(1, out),
    )
    return jnp.transpose(result, (1, 0, 2))


def solution(mesh):
    return jax.shard_map(
        functools.partial(local, mesh.shape["lon"]),
        mesh=mesh,
        in_specs=(P(None, ("grp", "lon"), None), P(None, "lon"), P(), P(), P(), P(), P()),
        out_specs=P(None, ("grp", "lon"), None),
        check_vma=False,
    )
```

time: 119 us -> 32.7 us (0.27)
  blocking collectives: 39.8 us -> 0 us
  local copies, waits for them, and re-layouts: 33.1 us -> 2.78 us
  Pallas kernels: 0 us -> 29.8 us
  matrix products: 27.8 us -> 0 us
  starting transfers between devices: 9.94 us -> 0 us
  other arithmetic: 7.89 us -> 0 us
    all_gather x2 -> x0, blocking collectives: 39.8 us -> none  [the longest x1 20.3 us: local(): top_state = lax.all_gather(masked[rows - 1], 'lon', axis=0, tiled=True)]
    pallas_call x0 -> x1, Pallas kernels: none -> 29.8 us  [local(): pl.pallas_call(kernel, out_shape=jax.ShapeDtypeStruct((width, rows, out),...]
    dot_general x18 -> x0, matrix products: 27.8 us -> none  [conv_taps(): jnp.dot(tap, weight[shift_y, shift_x], preferred_element_type=jnp.float32)]
    slice x13 -> x0, local copies, waits for them, and re-layouts: 23.5 us -> none  [the longest x9 21.9 us: conv_taps(): padded[shift_y:shift_y + rows, shift_x:shift_x + cols]]
    ppermute x4 -> x0, starting transfers between devices: 9.94 us -> none  [the longest x2 9.09 us: extended(): after = lax.ppermute(first, axis, down)]
    concatenate x3 -> x0, other arithmetic: 6.56 us -> none  [the longest x2 4.51 us: extended(): array = jnp.concatenate([before, array, after], axis=dim)]
    transpose x0 -> x1, local copies, waits for them, and re-layouts: none -> 2.78 us  [local(): return jnp.transpose(result, (1, 0, 2))]
    unnamed x33 -> x0, local copies, waits for them, and re-layouts: 2.55 us -> none
  transfers between devices with their start and end apart: 4 -> 0, of which waited for: 0 -> 0; matrix products, arithmetic and copies ran while one was open for 7% -> 0% of each run, Pallas kernels for 0% -> 0%
where the time goes in v1:
time: 32.7 us; the launch traced here: 32.6 us
  Pallas kernels  29.8 us (91%)
  local copies, waits for them, and re-layouts  2.78 us (9%)
    pallas_call x1, Pallas kernels, local(): pl.pallas_call(kernel, out_shape=jax.ShapeDtypeStruct((width, rows, out),...  29.8 us
    transpose x1, local copies, waits for them, and re-layouts, local(): return jnp.transpose(result, (1, 0, 2))  2.78 us

profile of v1, /device:TPU:0, one launch (start us, length us, event | category | flops | bytes accessed | tf_op | source)
XLA Modules:
  0.0 32.6 jit_solution(8986994172713141346)
XLA Ops:
  0.0 29.8 %masked_conv_pair.1 = bf16[8,256,256]{2,1,0:T(8,128)(2,1)} custom-call(bf16[300,8,256]{2,1,0:T(8,128)(2,1)} %bitcast.6, s32[8,256]{1,0:T(8,128)} %bitcast.7, s32[128]{0:T(128)} %fold_ref.1, bf16[3,3,300,256]{3,2,1,0:T(8,128)(2,1)} %w1_hbm.1, f32[1,256]{1,0:T(1,128)} %bitcast.8, bf16[3,3,256,256]{3,2,1,0:T(8,128)(2,1)} %w2_hbm.1, f32[1,256]{1,0:T(1,128)} %bitcast.9), custom_call_target="tpu_custom_call" | custom-call | tf_op jit(solution)/shard_map/masked_conv_pair/pallas_call | solution.py:232
  29.8 2.8 %copy.8 = bf16[256,8,256]{2,1,0:T(8,128)(2,1)} copy(bf16[256,8,256]{2,0,1:T(8,128)(2,1)} %bitcast.5) | data formatting | bytes 2097152 | tf_op jit(solution)/shard_map/transpose | solution.py:272

commit v2 on v1

--- a/solution.py
+++ b/solution.py
@@ -20,7 +20,7 @@
 
 def kernel(
     x_hbm, m_ref, fold_ref, w1_hbm, b1_ref, w2_hbm, b2_ref, out_ref,
-    xv, xs, w1, w2, wt, cols1, tails, cols2, top1, top2, mcol,
+    xv, xs, w1, w2, wt, cols1, tails, cols2, top1, top2, own1, all1, all2, part, pre, mcol,
     load_sem, t1_send, t1_recv, t2_send, t2_recv, x_send, x_recv, h_send, h_recv,
 ):
     n = lax.axis_size("lon")
@@ -75,10 +75,6 @@
         cols2[slot, :, 0:hid] = up.astype(BF16)
         cols2[slot, :, 2 * hid : 3 * hid] = down.astype(BF16)
 
-    def patch(buffer, slot, lo, hi, ghost):
-        old = buffer[slot, rows - 16 :, lo:hi].astype(F32)
-        buffer[slot, rows - 16 :, lo:hi] = jnp.where(last_tile, ghost, old).astype(BF16)
-
     def folded(top, slot):
         column = lax.rem(me * width + slot - 1 + total, total)
         return top[pl.ds(fold_ref[column], 1), :]
@@ -87,21 +83,19 @@
         lax.broadcasted_iota(jnp.int32, (1, padded), 1) < chans // 2, -1.0, 1.0
     )
 
-    def fold1(slot, _):
-        ghost = folded(top1, slot) * signs
-        patch(cols1, slot, 2 * main, 3 * main, ghost[:, :main])
-        patch(cols1, slot, 3 * main + LANES, 3 * main + 2 * LANES, ghost[:, main:])
-        return 0
-
-    def fold2(slot, _):
-        patch(cols2, slot, 2 * hid, 3 * hid, folded(top2, slot))
-        return 0
+    def ghosts(top):
+        lines = [folded(top, slot) for slot in range(width + 2)]
+        lines = lines + [jnp.zeros_like(lines[0])] * (2 * width - len(lines))
+        stack = jnp.concatenate(lines, axis=0)
+        return [stack[dx : dx + width] for dx in range(3)]
+
+    def twice(block):
+        return jnp.concatenate([block, block], axis=0).astype(BF16)
 
     def top_copy(top, send, recv, i):
         peer = lax.rem(me + i, n)
-        block = pl.ds(pl.multiple_of(me * width, width), width)
         return pltpu.make_async_remote_copy(
-            src_ref=top.at[block], dst_ref=top.at[block], send_sem=send.at[i],
+            src_ref=top.at[me], dst_ref=top.at[me], send_sem=send.at[i],
             recv_sem=recv.at[i], device_id={"lon": peer}, device_id_type=MESH,
         )
 
@@ -136,13 +130,12 @@
         )
         cols1[c + 1, :, main : 2 * main] = value[:, :main].astype(BF16)
         tails[c + 1] = value[:, main:].astype(BF16)
-        top1[pl.ds(me * width + c, 1), :] = value[rows - 1 :, :]
+        own1[pl.ds(c, 1), :] = value[rows - 1 :, :]
         build1(c + 1, value)
         return 0
 
     lax.fori_loop(0, width, spread, 0)
-    pl.semaphore_wait(barrier, n - 1)
-    send_tops(top1, t1_send, t1_recv)
+    top1[me] = own1[...].astype(BF16)
     mid1, mid2 = pl.ds(main, main), pl.ds(hid, hid)
     x_halos = [
         halo(cols1.at[1, :, mid1], cols1.at[width + 1, :, mid1], x_send, x_recv, 0, left),
@@ -150,76 +143,146 @@
         halo(cols1.at[width, :, mid1], cols1.at[0, :, mid1], x_send, x_recv, 2, right),
         halo(tails.at[width], tails.at[0], x_send, x_recv, 3, right),
     ]
-    for copy in x_halos:
-        copy.start()
-
     load_1.wait()
     for dx in range(3):
         for dy in range(3):
             wt[dx, TAIL_SLOT * dy : TAIL_SLOT * dy + chans - main, :] = w1[dy, dx, main:chans, :]
 
-    wait_tops(top1, t1_send, t1_recv)
-    lax.fori_loop(1, width + 1, fold1, 0)
-
-    def first(ca, cb):
+    tile = rows - 16
+
+    def weight1(dx):
+        return jnp.concatenate([w1[dy, dx, :main, :] for dy in range(3)] + [wt[dx]], axis=0)
+
+    def weight2(dx):
+        return jnp.concatenate([w2[dy, dx] for dy in range(3)], axis=0)
+
+    def dot(lhs, rhs):
+        return jnp.dot(lhs, rhs, preferred_element_type=F32)
+
+    def pair_of(buffer, weight, ca, cb):
         acc = None
         for dx in range(3):
-            lhs = jnp.concatenate([cols1[ca + dx], cols1[cb + dx]], axis=0)
-            rhs = jnp.concatenate([w1[dy, dx, :main, :] for dy in range(3)] + [wt[dx]], axis=0)
-            part = jnp.dot(lhs, rhs, preferred_element_type=F32)
-            acc = part if acc is None else acc + part
-        for k, c in enumerate((ca, cb)):
-            value = gelu(acc[k * rows : (k + 1) * rows] + b1_ref[...]) * mcol[c]
-            value = value.astype(BF16)
-            cols2[c + 1, :, hid : 2 * hid] = value
-            value = value.astype(F32)
-            top2[pl.ds(me * width + c, 1), :] = value[rows - 1 :, :]
-            build2(c + 1, value)
+            lhs = jnp.concatenate([buffer[ca + dx], buffer[cb + dx]], axis=0)
+            term = dot(lhs, weight(dx))
+            acc = term if acc is None else acc + term
+        return acc
+
+    def edges_of(buffer, weight):
+        both = jnp.concatenate([buffer[1], buffer[width]], axis=0)
+        acc = dot(both, weight(1))
+        part[0] = acc[:rows] + dot(buffer[2], weight(2))
+        part[1] = acc[rows:] + dot(buffer[width - 1], weight(0))
+
+    def activate(c, value):
+        value = (gelu(value) * mcol[c]).astype(BF16)
+        cols2[c + 1, :, hid : 2 * hid] = value
+        value = value.astype(F32)
+        build2(c + 1, value)
+
+    def first(ca, cb):
+        acc = pair_of(cols1, weight1, ca, cb) + b1_ref[...]
+        pre[pl.ds(ca, 1), :] = acc[rows - 1 : rows, :]
+        pre[pl.ds(cb, 1), :] = acc[2 * rows - 1 :, :]
+        activate(ca, acc[:rows])
+        activate(cb, acc[rows:])
+
+    def edge(buffer, weight, side):
+        slot, dx = ((0, 0), (width + 1, 2))[side]
+        return part[side] + dot(buffer[slot], weight(dx))
+
+    mask_top = mask[:, rows - 1 :]
+
+    def first_edge(side):
+        c = side * (width - 1)
+        acc = edge(cols1, weight1, side) + b1_ref[...]
+        pre[c : c + 1, :] = acc[rows - 1 :, :]
+        activate(c, acc)
+
+    def first_top():
+        fold = [g * signs for g in ghosts(all1)]
+        extra = pre[...]
+        for dx in range(3):
+            extra = extra + dot(twice(fold[dx][:, :main]), w1[2, dx, :main, :])[:width]
+            extra = extra + dot(twice(fold[dx][:, main:]), wt[dx, LANES:, :])[:width]
+        hidden = (gelu(extra) * mask_top).astype(BF16).astype(F32)
+        top2[me] = hidden.astype(BF16)
+        for c in range(width):
+            old = cols2[c + 1, tile:, hid : 2 * hid].astype(F32)
+            value = jnp.where(last_tile, hidden[c : c + 1], old)
+            cols2[c + 1, tile:, hid : 2 * hid] = value.astype(BF16)
+            down = jnp.where(last_tile, 0.0, pltpu.roll(value, 15, 0))
+            cols2[c + 1, tile:, 2 * hid : 3 * hid] = down.astype(BF16)
+
+    def put(c, value):
+        for h in range(hid // LANES):
+            part = value[:, h * LANES : (h + 1) * LANES]
+            xs[h, pl.ds(c, rows, stride=width), :] = part
 
     def second(ca, cb):
-        acc = None
+        acc = pair_of(cols2, weight2, ca, cb) + b2_ref[...]
+        put(ca, acc[:rows] * mcol[ca])
+        put(cb, acc[rows:] * mcol[cb])
+
+    def second_edge(side):
+        c = side * (width - 1)
+        put(c, (edge(cols2, weight2, side) + b2_ref[...]) * mcol[c])
+
+    def second_top():
+        fold = ghosts(all2)
+        extra = None
         for dx in range(3):
-            lhs = jnp.concatenate([cols2[ca + dx], cols2[cb + dx]], axis=0)
-            rhs = jnp.concatenate([w2[dy, dx] for dy in range(3)], axis=0)
-            part = jnp.dot(lhs, rhs, preferred_element_type=F32)
-            acc = part if acc is None else acc + part
-        for k, c in enumerate((ca, cb)):
-            value = (acc[k * rows : (k + 1) * rows] + b2_ref[...]) * mcol[c]
-            out_ref[c] = value.astype(BF16)
-
-    def inner(step):
+            term = dot(twice(fold[dx]), w2[2, dx])[:width]
+            extra = term if extra is None else extra + term
+        extra = extra * mask_top
+        for h in range(hid // LANES):
+            at = (rows - 1) * width
+            xs[h, at : at + width, :] += extra[:, h * LANES : (h + 1) * LANES]
+
+    def inner(step, lo, hi):
         def one(i, _):
             step(2 * i + 1, 2 * i + 2)
             return 0
 
-        lax.fori_loop(0, (width - 2) // 2, one, 0)
-
-    inner(first)
+        lax.fori_loop(lo, hi, one, 0)
+
+    pairs = (width - 2) // 2
+    pl.semaphore_wait(barrier, n - 1)
+    send_tops(top1, t1_send, t1_recv)
+    for copy in x_halos:
+        copy.start()
+    edges_of(cols1, weight1)
+    inner(first, 0, pairs)
+    wait_tops(top1, t1_send, t1_recv)
+    all1[...] = top1[...].astype(F32).reshape(all1.shape)
     for copy in x_halos:
         copy.wait()
-    for slot in (0, width + 1):
+    for side, slot in enumerate((0, width + 1)):
         mid = jnp.concatenate([cols1[slot, :, main : 2 * main], tails[slot]], axis=1)
         build1(slot, mid.astype(F32))
-        fold1(slot, 0)
-    first(0, width - 1)
-
-    send_tops(top2, t2_send, t2_recv)
+        first_edge(side)
+    first_top()
+
     h_halos = [
         halo(cols2.at[1, :, mid2], cols2.at[width + 1, :, mid2], h_send, h_recv, 0, left),
         halo(cols2.at[width, :, mid2], cols2.at[0, :, mid2], h_send, h_recv, 1, right),
     ]
+    send_tops(top2, t2_send, t2_recv)
     for copy in h_halos:
         copy.start()
     load_2.wait()
+    edges_of(cols2, weight2)
+    inner(second, 0, pairs)
     wait_tops(top2, t2_send, t2_recv)
-    lax.fori_loop(1, width + 1, fold2, 0)
-    inner(second)
+    all2[...] = top2[...].astype(F32).reshape(all2.shape)
     for copy in h_halos:
         copy.wait()
-    for slot in (0, width + 1):
+    for side, slot in enumerate((0, width + 1)):
         build2(slot, cols2[slot, :, hid : 2 * hid].astype(F32))
-        fold2(slot, 0)
-    second(0, width - 1)
+        second_edge(side)
+    second_top()
+    for h in range(hid // LANES):
+        block = xs[h, 0 : rows * width, :].reshape(rows, width, LANES)
+        out_ref[:, :, h * LANES : (h + 1) * LANES] = block.astype(BF16)
 
 
 def local(n, state, ocean_mask, fold_map, w_first, b_first, w_second, b_second):
@@ -231,7 +294,7 @@
     hbm = pl.BlockSpec(memory_space=pl.ANY)
     result = pl.pallas_call(
         kernel,
-        out_shape=jax.ShapeDtypeStruct((width, rows, out), BF16),
+        out_shape=jax.ShapeDtypeStruct((rows, width, out), BF16),
         in_specs=[hbm, vmem, pl.BlockSpec(memory_space=pltpu.SMEM), hbm, vmem, hbm, vmem],
         out_specs=vmem,
         scratch_shapes=[
@@ -243,8 +306,13 @@
             pltpu.VMEM((width + 2, rows, 3 * main + 2 * LANES), BF16),
             pltpu.VMEM((width + 2, rows, LANES), BF16),
             pltpu.VMEM((width + 2, rows, 3 * hid), BF16),
+            pltpu.VMEM((n, width, main + LANES), BF16),
+            pltpu.VMEM((n, width, hid), BF16),
+            pltpu.VMEM((width, main + LANES), F32),
             pltpu.VMEM((n * width, main + LANES), F32),
             pltpu.VMEM((n * width, hid), F32),
+            pltpu.VMEM((2, rows, hid), F32),
+            pltpu.VMEM((width, hid), F32),
             pltpu.VMEM((width, rows, 1), F32),
             pltpu.SemaphoreType.DMA((3,)),
             pltpu.SemaphoreType.DMA((n,)),
@@ -269,7 +337,7 @@
         w_second,
         b_second.reshape(1, out),
     )
-    return jnp.transpose(result, (1, 0, 2))
+    return result
 
 
 def solution(mesh):

time: 32.7 us -> 25 us (0.76)
  Pallas kernels: 29.8 us -> 22.3 us
  local copies, waits for them, and re-layouts: 2.78 us -> 2.26 us
    pallas_call x1, Pallas kernels: 29.8 us -> 22.3 us  [local(): pl.pallas_call(kernel, out_shape=jax.ShapeDtypeStruct((rows, width, out),...]
    transpose x1 -> x0, local copies, waits for them, and re-layouts: 2.78 us -> none  [local(): return jnp.transpose(result, (1, 0, 2))]
    unnamed x0 -> x1, local copies, waits for them, and re-layouts: none -> 2.26 us
where the time goes in v2:
time: 25 us; the launch traced here: 24.6 us
  Pallas kernels  22.3 us (89%)
  local copies, waits for them, and re-layouts  2.26 us (9%)
    pallas_call x1, Pallas kernels, local(): pl.pallas_call(kernel, out_shape=jax.ShapeDtypeStruct((rows, width, out),...  22.3 us
    unnamed x1, local copies, waits for them, and re-layouts  2.26 us

profile of v2, /device:TPU:0, one launch (start us, length us, event | category | flops | bytes accessed | tf_op | source)
XLA Modules:
  0.0 24.6 jit_solution(8444870482084691571)
XLA Ops:
  0.0 22.3 %masked_conv_pair.1 = bf16[256,8,256]{2,1,0:T(8,128)(2,1)} custom-call(bf16[300,8,256]{2,1,0:T(8,128)(2,1)} %bitcast.4, s32[8,256]{1,0:T(8,128)} %bitcast.5, s32[128]{0:T(128)} %fold_ref.1, bf16[3,3,300,256]{3,2,1,0:T(8,128)(2,1)} %w1_hbm.1, f32[1,256]{1,0:T(1,128)} %bitcast.6, bf16[3,3,256,256]{3,2,1,0:T(8,128)(2,1)} %w2_hbm.1, f32[1,256]{1,0:T(1,128)} %bitcast.7), custom_call_target="tpu_custom_call" | custom-call | tf_op jit(solution)/shard_map/masked_conv_pair/pallas_call | solution.py:295
  22.4 2.3 %copy.9 = bf16[256,8,256]{2,1,0:T(8,128)(2,1)} copy(bf16[256,8,256]{2,1,0:T(8,128)(2,1)} %masked_conv_pair.1) | data formatting | bytes 2097152

commit v3 on v2

--- a/solution.py
+++ b/solution.py
@@ -283,6 +283,36 @@
     for h in range(hid // LANES):
         block = xs[h, 0 : rows * width, :].reshape(rows, width, LANES)
         out_ref[:, :, h * LANES : (h + 1) * LANES] = block.astype(BF16)
+
+
+def move(parts, src, dst, held, sems_in, sems_out):
+    step = src.shape[0] // parts
+    loads, stores = [], []
+    for i in range(parts):
+        at = pl.ds(i * step, step)
+        loads.append(pltpu.make_async_copy(src.at[at], held.at[at], sems_in.at[i]))
+        stores.append(pltpu.make_async_copy(held.at[at], dst.at[at], sems_out.at[i]))
+        loads[-1].start()
+    for load, store in zip(loads, stores):
+        load.wait()
+        store.start()
+    for store in stores:
+        store.wait()
+
+
+def handed_on(array, parts):
+    return pl.pallas_call(
+        functools.partial(move, parts),
+        out_shape=jax.ShapeDtypeStruct(array.shape, array.dtype),
+        in_specs=[pl.BlockSpec(memory_space=pl.ANY)],
+        out_specs=pl.BlockSpec(memory_space=pl.ANY),
+        scratch_shapes=[
+            pltpu.VMEM(array.shape, array.dtype),
+            pltpu.SemaphoreType.DMA((parts,)),
+            pltpu.SemaphoreType.DMA((parts,)),
+        ],
+        name="hand_on",
+    )(array)
 
 
 def local(n, state, ocean_mask, fold_map, w_first, b_first, w_second, b_second):
@@ -337,7 +367,7 @@
         w_second,
         b_second.reshape(1, out),
     )
-    return result
+    return handed_on(result, 4)
 
 
 def solution(mesh):

time: 25 us -> 24.7 us (0.988)
  local copies, waits for them, and re-layouts: 2.26 us -> 0 us
  Pallas kernels: 22.3 us -> 24.3 us
    unnamed x1 -> x0, local copies, waits for them, and re-layouts: 2.26 us -> none
    pallas_call x0 -> x1, Pallas kernels: none -> 1.98 us  [handed_on(): pl.pallas_call(functools.partial(move, parts), out_shape=jax.ShapeDtypeSt...]
where the time goes in v3:
time: 24.7 us; the launch traced here: 24.3 us
  Pallas kernels  24.3 us (98%)
    pallas_call x1, Pallas kernels, local(): pl.pallas_call(kernel, out_shape=jax.ShapeDtypeStruct((rows, width, out),...  22.3 us
    pallas_call x1, Pallas kernels, handed_on(): pl.pallas_call(functools.partial(move, parts), out_shape=jax.ShapeDtypeSt...  1.98 us

profile of v3, /device:TPU:0, one launch (start us, length us, event | category | flops | bytes accessed | tf_op | source)
XLA Modules:
  0.0 24.3 jit_solution(1192915863926630358)
XLA Ops:
  0.0 22.3 %masked_conv_pair.1.src = bf16[256,8,256]{2,1,0:T(8,128)(2,1)} custom-call(bf16[300,8,256]{2,1,0:T(8,128)(2,1)} %bitcast.4, s32[8,256]{1,0:T(8,128)} %bitcast.5, s32[128]{0:T(128)} %fold_ref.1, bf16[3,3,300,256]{3,2,1,0:T(8,128)(2,1)} %w1_hbm.1, f32[1,256]{1,0:T(1,128)} %bitcast.6, bf16[3,3,256,256]{3,2,1,0:T(8,128)(2,1)} %w2_hbm.1, f32[1,256]{1,0:T(1,128)} %bitcast.7), custom_call_target="tpu_custom_call" | custom-call | tf_op jit(solution)/shard_map/masked_conv_pair/pallas_call | solution.py:325
  22.4 2.0 %hand_on.1 = bf16[256,8,256]{2,1,0:T(8,128)(2,1)} custom-call(bf16[256,8,256]{2,1,0:T(8,128)(2,1)} %masked_conv_pair.1.src), custom_call_target="tpu_custom_call" | custom-call | tf_op jit(solution)/shard_map/hand_on/pallas_call | solution.py:304
